TPU v7x, 256 devices: a whole 4x4x8 slice. The times are simulated.
256 devices in a mesh: head: 4 (over x), inner: 16 (over z, core), outer: 4 (over y).
Axes of the slice: x: 4, y: 4, z: 8, core: 2. Of those that a mesh axis runs over, the one named last changes fastest.
Arguments:
- queries: bfloat16 [8192, 64, 128], P(('outer', 'inner'), None, 'head'), may hold values from -6 to 6
- keys: bfloat16 [8192, 8, 128], P(('outer', 'inner'), None, 'head'), may hold values from -6 to 6
- values: bfloat16 [8192, 8, 128], P(('outer', 'inner'), None, 'head'), may hold values from -6 to 6
- grad_out: bfloat16 [8192, 64, 128], P(('outer', 'inner'), None, 'head'), may hold values from -6 to 6
- span_order: int32 [128], replicated, may hold values from 0 to 127, as said below
- doc_ids: int32 [8192], replicated, may hold values from 0 to 3, never falling along the last dimension, each value on 1 to 4096 neighbouring positions
Outputs:
- attn_out: bfloat16 [8192, 64, 128], P(('outer', 'inner'), 'head')
- query_grads: float32 [8192, 64, 128], P(('outer', 'inner'), 'head')
- key_grads: float32 [8192, 8, 128], P(('outer', 'inner'), 'head')
- value_grads: float32 [8192, 8, 128], P(('outer', 'inner'), 'head')
Inputs may be any that keep to these rules, and one draw needn't show every extreme that they name: `span_order`: stored span slots 2r and 2r+1 hold the spans c and 127 - c for some c; every span appears once. doc_ids never falls along the sequence.
All inputs are finite; a program needn't handle non-finite values.
Results may differ from a plain program's by a relative error of at most 0.025.
Values may be sent and summed in bfloat16 or wider, within the bound.
A program may use at most 64 MiB of HBM per device.

v0:
```python
import functools
import math

import jax
import jax.numpy as jnp
from jax import lax
from jax.experimental import pallas as pl
from jax.experimental.pallas import tpu as pltpu
from jax.sharding import PartitionSpec as P

MESH = pl.DeviceIdType.MESH
HBM = pl.BlockSpec(memory_space=pltpu.HBM)
NEG = -1e30
FAR = 1 << 24
NX = 4
NY = 4
NZ = 8
HD = 128
ROWS = 128
SPAN = 64
GROUP = 8
SLOTS = 64
LANES = GROUP * SPAN
SCALE = 1.0 / math.sqrt(HD)
LOG2E = math.log2(math.e)
ITEM = 4
BF16 = jnp.bfloat16
F32 = jnp.float32


def place():
    inner = lax.axis_index("inner")
    return (
        lax.axis_index("head"),
        lax.axis_index("outer"),
        lax.div(inner, 2),
        lax.rem(inner, 2),
    )


def where_is(x, y, z, core):
    return {"head": x, "outer": y, "inner": z * 2 + core}


def greet(partners):
    barrier = pltpu.get_barrier_semaphore()
    for partner in partners:
        pl.semaphore_signal(barrier, inc=1, device_id=partner, device_id_type=MESH)
    pl.semaphore_wait(barrier, len(partners))


def send(src, dst, send_sem, recv_sem, partner):
    copy = pltpu.make_async_remote_copy(
        src_ref=src,
        dst_ref=dst,
        send_sem=send_sem,
        recv_sem=recv_sem,
        device_id=partner,
        device_id_type=MESH,
    )
    copy.start()
    return copy


def bring_kernel(
    q, k, v, g, q_cols_out, g_cols_out, q_rows_out, g_rows_out, kv_out,
    q_cols, g_cols, q_rows, g_rows, out_sem, q_in, g_in, kv_in, ring_kv, relay, relay_sem, own_sem, keep_sem, x_send, x_recv, y_send, y_recv, z_send, z_recv,
):
    x, y, z, core = place()
    peers = [(dx, dc) for dx in range(NX) for dc in range(2) if (dx, dc) != (0, 0)]

    def peer(dx, dc):
        return where_is(lax.rem(x + dx, NX), y, z, lax.rem(core + dc, 2))

    up = where_is(x, y, lax.rem(z + 1, NZ), core)
    down = where_is(x, y, lax.rem(z + NZ - 1, NZ), core)
    later = where_is(x, lax.rem(y + 1, NY), z, core)
    earlier = where_is(x, lax.rem(y + NY - 1, NY), z, core)
    up_z, down_z = lax.rem(z + 1, NZ), lax.rem(z + NZ - 1, NZ)
    later_y, earlier_y = lax.rem(y + 1, NY), lax.rem(y + NY - 1, NY)
    corners = (where_is(x, later_y, up_z, core), where_is(x, later_y, down_z, core))
    behind = [where_is(x, earlier_y, up_z, core), where_is(x, earlier_y, down_z, core)]
    greet([peer(*p) for p in peers] + [up, down, later, earlier, *corners, *behind])

    here = pl.ds(pl.multiple_of(x * 32, 32), 32)
    copies = []
    own = []
    for index, (dx, dc) in enumerate([(0, 0)] + peers):
        head = lax.rem(x + dx, NX) * 2 + lax.rem(core + dc, 2)
        for kind, src in enumerate((k, v)):
            dst = kv_in.at[kind, core, here]
            if index == 0:
                copy = pltpu.make_async_copy(src.at[head], dst, own_sem.at[kind])
                copy.start()
                own.append(copy)
            else:
                copies.append(
                    send(src.at[head], dst, x_send.at[kind, index], x_recv.at[kind, index], peer(dx, dc))
                )
    own[0].wait()
    own[1].wait()
    for copy in copies:
        copy.wait()
    for kind in range(2):
        for block in range(2):
            ring_kv[z, kind, block * ROWS : (block + 1) * ROWS, :] = (
                kv_in[kind, block].astype(F32).T.astype(BF16)
            )
    keeps = []
    sent = []
    ways = (up, down)

    def block_at(group, way, step):
        return group * NZ + lax.rem(z + NZ + step * (1 if way else -1), NZ)

    def keep(block, index):
        copy = pltpu.make_async_copy(ring_kv.at[block], kv_out.at[block], keep_sem.at[index])
        copy.start()
        keeps.append(copy)

    def hop(group, way, step, kind):
        block = block_at(group, way, step - 1)
        copy = send(
            ring_kv.at[block, kind], ring_kv.at[block, kind],
            z_send.at[group, way, step - 1, kind], z_recv.at[group, way, step - 1, kind],
            ways[way],
        )
        sent.append(copy)
        return copy

    def shift(way, step, kind):
        block = block_at(0, way, min(step, 3))
        copy = send(
            ring_kv.at[block, kind], ring_kv.at[NZ + block, kind],
            y_send.at[way, step, kind], y_recv.at[way, step, kind],
            corners[way] if step == 4 else later,
        )
        sent.append(copy)
        return copy

    def settle(kind):
        src, cols, rows = ((q_in, q_cols, q_rows), (g_in, g_cols, g_rows))[kind]
        own[2 + kind].wait()
        for copy in wide[kind]:
            copy.wait()
        low = lax.broadcasted_iota(jnp.int32, (HD, ROWS), 1) < SPAN

        @pl.loop(0, 8)
        def _(index):
            block = lax.div(index, 4)
            pair = lax.rem(index, 4)
            lanes = pl.ds(pl.multiple_of(pair * ROWS, ROWS), ROWS)
            first, second = [
                jnp.concatenate([src[block, a, 2 * pair + b] for a in range(NX)], axis=0).astype(F32)
                for b in range(2)
            ]
            halves = (
                jnp.where(low, first, pltpu.roll(second, SPAN, 1)),
                jnp.where(low, pltpu.roll(first, SPAN, 1), second),
            )
            for half in range(2):
                cols[2 * block + half, :, lanes] = halves[half].astype(BF16)
                rows[2 * block + half, lanes, :] = halves[half].T.astype(BF16)

        outs = ((q_cols_out, q_rows_out), (g_cols_out, g_rows_out))[kind]
        for index, (src, dst) in enumerate(zip((cols, rows), outs)):
            copy = pltpu.make_async_copy(src, dst, out_sem.at[kind, index])
            copy.start()
            own.append(copy)

    near = {}
    self_shift = {}
    for kind in range(2):
        for way in range(2):
            near[way, 1, kind] = hop(0, way, 1, kind)
        self_shift[kind] = shift(0, 0, kind)
    keep(z, 0)
    heads = pl.ds((x * 2 + core) * GROUP, GROUP)
    for kind, (src, dst) in enumerate(((q, q_in), (g, g_in))):
        copy = pltpu.make_async_copy(
            src.at[heads], dst.at[core, x], own_sem.at[2 + kind]
        )
        copy.start()
        own.append(copy)
    wide = ([], [])
    relays = []
    for kind, src in enumerate((q, g)):
        relays.append(
            send(
                src.at[pl.ds(lax.rem(x + 2, NX) * 2 * GROUP, 2 * GROUP)], relay.at[kind],
                relay_sem.at[0, kind], relay_sem.at[1, kind], peer(3 if kind else 1, 0),
            )
        )
    for kind, (src, dst) in enumerate(((q, q_in), (g, g_in))):
        for index, (dx, dc) in enumerate(peers):
            if dx == 2:
                continue
            head = lax.rem(x + dx, NX) * 2 + lax.rem(core + dc, 2)
            wide[kind].append(
                send(
                    src.at[pl.ds(head * GROUP, GROUP)],
                    dst.at[core, x],
                    x_send.at[2 + kind, index],
                    x_recv.at[2 + kind, index],
                    peer(dx, dc),
                )
            )
    def forward(kind):
        relays[kind].wait_recv()
        from_x = lax.rem(x + (1 if kind else 3), NX)
        for index, (dx, dc) in enumerate(peers):
            if dx != 2:
                continue
            head = pl.ds(lax.rem(core + dc, 2) * GROUP, GROUP)
            wide[kind].append(
                send(
                    relay.at[kind, head],
                    (q_in, g_in)[kind].at[core, from_x],
                    x_send.at[2 + kind, index],
                    x_recv.at[2 + kind, index],
                    peer(3 if kind else 1, dc),
                )
            )

    far_shift = {}
    for step in range(1, 4):
        for kind in range(2):
            for way in range(2):
                near[way, step, kind].wait_recv()
                if step < 3 or kind == way:
                    near[way, step + 1, kind] = hop(0, way, step + 1, kind)
                if step == 3 and kind == way:
                    far_shift[way, 4] = shift(way, 4, way)
                if step == 2 or (step == 1 and kind == way):
                    far_shift[way, step, kind] = shift(way, step, kind)
        for way in range(2):
            keep(block_at(0, way, step), 1 + 2 * step + way)
        if step == 1:
            forward(0)
            forward(1)
    hops = {}
    for kind in range(2):
        self_shift[kind].wait_recv()
        hops[1 - kind, 1, kind] = hop(1, 1 - kind, 1, kind)
    keep(NZ + z, 1)
    for kind in range(2):
        for way in range(2):
            far_shift[way, 2, kind].wait_recv()
            hops[way, 3, kind] = hop(1, way, 3, kind)
    for way in range(2):
        keep(block_at(1, way, 2), 9 + way)
    settle(0)
    settle(1)
    for way in range(2):
        near[way, 4, way].wait_recv()
    keep(block_at(0, 0, 4), 2)
    for step in (1, 3):
        for way in range(2):
            for kind in range(2):
                arriving = far_shift if step == 1 and kind == way else hops
                arriving[way, step, kind].wait_recv()
            keep(block_at(1, way, step), 10 + step + way)
    for way in range(2):
        far_shift[way, 4].wait_recv()
    keep(block_at(1, 0, 4), 15)
    for copy in sent + relays:
        copy.wait_send()
    for copy in keeps:
        copy.wait()
    for copy in own[4:]:
        copy.wait()


def bring(q, k, v, g):
    return pl.pallas_call(
        bring_kernel,
        out_shape=(
            jax.ShapeDtypeStruct((4, HD, LANES), BF16),
            jax.ShapeDtypeStruct((4, HD, LANES), BF16),
            jax.ShapeDtypeStruct((4, LANES, HD), BF16),
            jax.ShapeDtypeStruct((4, LANES, HD), BF16),
            jax.ShapeDtypeStruct((2 * NZ, 2, 2 * ROWS, HD), BF16),
        ),
        in_specs=[HBM] * 4,
        out_specs=(HBM,) * 5,
        scratch_shapes=[
            pltpu.VMEM((4, HD, LANES), BF16),
            pltpu.VMEM((4, HD, LANES), BF16),
            pltpu.VMEM((4, LANES, HD), BF16),
            pltpu.VMEM((4, LANES, HD), BF16),
            pltpu.SemaphoreType.DMA((2, 2)),
            pltpu.VMEM((2, NX, GROUP, HD // NX, ROWS), BF16),
            pltpu.VMEM((2, NX, GROUP, HD // NX, ROWS), BF16),
            pltpu.VMEM((2, 2, HD, ROWS), BF16),
            pltpu.VMEM((2 * NZ, 2, 2 * ROWS, HD), BF16),
            pltpu.VMEM((2, 2 * GROUP, HD // NX, ROWS), BF16),
            pltpu.SemaphoreType.DMA((2, 2)),
            pltpu.SemaphoreType.DMA((4,)),
            pltpu.SemaphoreType.DMA((16,)),
            pltpu.SemaphoreType.DMA((4, 8)),
            pltpu.SemaphoreType.DMA((4, 8)),
            pltpu.SemaphoreType.DMA((2, 5, 2)),
            pltpu.SemaphoreType.DMA((2, 5, 2)),
            pltpu.SemaphoreType.DMA((2, 2, 4, 2)),
            pltpu.SemaphoreType.DMA((2, 2, 4, 2)),
        ],
        compiler_params=pltpu.CompilerParams(
            collective_id=0, has_side_effects=True, vmem_limit_bytes=60 << 20
        ),
        name="bring",
    )(q, k, v, g)


def attend_kernel(
    order_in, docs_in, q_cols_in, g_cols_in, q_rows_in, g_rows_in, kv_in, both_out, dkv,
    order, docs, q_cols, g_cols, q_rows, g_rows, both, dq, kv, scores, key_acc, value_acc, out_acc, tops, sums, shift, dots,
    pos_rows, start_rows, item_list, span_list, in_sem, out_sem,
):
    outer = lax.axis_index("outer")
    chip = lax.div(lax.axis_index("inner"), 2)
    loads = [
        pltpu.make_async_copy(order_in, order, in_sem.at[0]),
        pltpu.make_async_copy(docs_in, docs, in_sem.at[1]),
        pltpu.make_async_copy(q_cols_in, q_cols, in_sem.at[2]),
        pltpu.make_async_copy(kv_in.at[:, 0], kv.at[pl.ds(0, 2 * NZ), 0], in_sem.at[3]),
        pltpu.make_async_copy(kv_in.at[:, 1], kv.at[pl.ds(0, 2 * NZ), 1], in_sem.at[4]),
        pltpu.make_async_copy(g_cols_in, g_cols, in_sem.at[5]),
        pltpu.make_async_copy(q_rows_in, q_rows, in_sem.at[6]),
        pltpu.make_async_copy(g_rows_in, g_rows, in_sem.at[7]),
    ]
    for load in loads:
        load.start()
    kv[2 * NZ] = jnp.zeros((2, 4, SPAN, HD), BF16)
    tops[...] = jnp.full_like(tops, NEG)
    sums[...] = jnp.zeros_like(sums)
    loads[0].wait()
    loads[1].wait()
    doc = docs[...]
    starts = [
        jnp.sum(jnp.where(doc < d, 1.0, 0.0)).astype(jnp.int32) for d in range(1, 4)
    ]

    def start_of(position):
        found = jnp.zeros_like(position)
        for start in starts:
            found = jnp.where(position >= start, jnp.maximum(found, start), found)
        return found

    iota_lanes = lax.rem(lax.broadcasted_iota(jnp.int32, (8, ROWS), 1), SPAN)
    lows = []
    highs = []
    for unit in range(4):
        query_span = order[outer * 32 + chip * 4 + unit]
        lows.append(lax.div(start_of(query_span * SPAN), SPAN))
        highs.append(query_span)
        query_pos = query_span * SPAN + iota_lanes
        pos_rows[unit] = query_pos
        start_rows[unit] = start_of(query_pos)

    counts = tuple(jnp.int32(unit * 128) for unit in range(4))
    for group in range(2):
        stored = lax.rem(outer + 4 - group, 4) * 32

        def note(step, counts):
            for part in range(8):
                slot = step * 8 + part
                span = order[stored + slot]
                entry = span * (2 * SPAN) + (group * 32 + slot)
                new = []
                for unit in range(4):
                    span_list[counts[unit]] = entry
                    allowed = (span >= lows[unit]) & (span <= highs[unit])
                    new.append(counts[unit] + jnp.where(allowed, 1, 0))
                counts = tuple(new)
            nothing = jnp.zeros((8, SPAN, HD), F32)
            rows = pl.ds((group * 4 + step) * 8, 8)
            key_acc[rows] = nothing
            value_acc[rows] = nothing
            flat = pl.ds(pl.multiple_of(step * 32, 32), 32)
            for unit in range(2 * group, 2 * group + 2):
                out_acc[unit, flat, :] = jnp.zeros((32, LANES), F32)
                dq[unit, flat, :] = jnp.zeros((32, LANES), F32)
            return counts

        counts = lax.fori_loop(0, 4, note, counts)
    items = jnp.int32(0)
    for unit in range(4):
        for extra in range(ITEM):
            span_list[counts[unit] + extra] = 2 * FAR + SLOTS
        for chunk in range(SLOTS // ITEM):
            item_list[items + chunk] = unit * 128 + chunk * ITEM
        items = items + lax.div(counts[unit] - unit * 128 + ITEM - 1, ITEM)
    blank = 3 * 128 + 72
    for extra in range(ITEM):
        span_list[blank + extra] = 2 * FAR + SLOTS
    for extra in range(4):
        item_list[items + extra] = blank
    steps = lax.div(items + 3, 4)

    iota_keys = (
        lax.broadcasted_iota(jnp.int32, (8, 8, ROWS), 0) * 8
        + lax.broadcasted_iota(jnp.int32, (8, 8, ROWS), 1)
    )

    def entries(item):
        first = item_list[item]
        found = [span_list[first + part] for part in range(ITEM)]
        slots = [lax.rem(entry, 2 * SPAN) for entry in found]
        return lax.div(first, 128), slots, [lax.div(a - b, 2) for a, b in zip(found, slots)]

    def spans(slots, kind):
        parts = []
        for slot in slots:
            parts.append(kv[lax.div(slot, 4), kind, lax.rem(slot, 4)])
        return jnp.concatenate(parts, axis=0)

    sides = [pl.ds(side * 256, 256) for side in range(2)]
    loads[2].wait()
    loads[3].wait()

    @functools.partial(lax.fori_loop, 0, steps, init_val=0)
    def _(step, _):
        results = []
        for item in [4 * step + part for part in range(4)]:
            unit, slots, bases = entries(item)
            keys = spans(slots, 0)
            biases = []
            for base in bases:
                allowed = (iota_keys <= (pos_rows[unit] - base)[None]) & (
                    iota_keys >= (start_rows[unit] - base)[None]
                )
                biases.append(jnp.where(allowed, 0.0, NEG).reshape(SPAN, ROWS))
            bias = jnp.concatenate(biases, axis=0)
            bias = jnp.concatenate([bias, bias], axis=1)
            for lanes in sides:
                tile = jnp.dot(keys, q_cols[unit, :, lanes], preferred_element_type=F32)
                tile = tile * (SCALE * LOG2E) + bias
                scores[item, :, lanes] = tile
                results.append((unit, lanes, jnp.max(tile.reshape(32, 8, 256), axis=0)))
        for unit, lanes, top in results:
            tops[unit, :, lanes] = jnp.maximum(tops[unit, :, lanes], top)
        return 0

    for unit in range(4):
        shift[unit] = jnp.broadcast_to(jnp.max(tops[unit], axis=0, keepdims=True), (8, LANES))
    loads[4].wait()

    @functools.partial(lax.fori_loop, 0, steps, init_val=0)
    def _(step, _):
        results = []
        for item in [4 * step + part for part in range(4)]:
            unit, slots, _ = entries(item)
            values_t = spans(slots, 1).T
            for lanes in sides:
                logits = scores[item, :, lanes].reshape(32, 8, 256)
                probs = jnp.exp2(logits - shift[unit, :, lanes][None])
                part = jnp.dot(
                    values_t, probs.reshape(256, 256).astype(BF16), preferred_element_type=F32
                )
                results.append((unit, lanes, jnp.sum(probs, axis=0), part))
        for unit, lanes, total, part in results:
            sums[unit, :, lanes] += total
            out_acc[unit, :, lanes] += part
        return 0

    for load in loads[5:]:
        load.wait()
    for unit in range(4):
        row_sum = jnp.sum(sums[unit], axis=0, keepdims=True)
        out = (out_acc[unit] * (1.0 / row_sum)).astype(BF16)
        both[unit, 0] = out
        row_dot = jnp.sum(
            out.astype(F32) * g_cols[unit].astype(F32), axis=0, keepdims=True
        )
        dots[unit] = jnp.broadcast_to(row_dot, (8, LANES))
        shift[unit] = shift[unit] + jnp.log(row_sum) * LOG2E

    @functools.partial(lax.fori_loop, 0, steps, init_val=0)
    def _(step, _):
        results = []
        for item in [4 * step + part for part in range(4)]:
            unit, slots, _ = entries(item)
            keys_t = spans(slots, 0).T
            values = spans(slots, 1)
            probs_b = []
            score_grads = []
            for lanes in sides:
                logits = scores[item, :, lanes].reshape(32, 8, 256)
                probs = jnp.exp2(logits - shift[unit, :, lanes][None])
                steep = jnp.dot(values, g_cols[unit, :, lanes], preferred_element_type=F32)
                steep = probs * (steep.reshape(32, 8, 256) - dots[unit, :, lanes][None])
                probs_b.append(probs.reshape(256, 256).astype(BF16))
                score_grads.append(steep.reshape(256, 256).astype(BF16))
            probs_b = jnp.concatenate(probs_b, axis=1)
            score_grads = jnp.concatenate(score_grads, axis=1)
            to_values = jnp.dot(probs_b, g_rows[unit], preferred_element_type=F32)
            to_keys = jnp.dot(score_grads, q_rows[unit], preferred_element_type=F32)
            to_query = jnp.dot(keys_t, score_grads, preferred_element_type=F32)
            results.append((slots, unit, to_values, to_keys, to_query))
        for slots, unit, to_values, to_keys, to_query in results:
            dq[unit] += to_query
            for acc, part in ((key_acc, to_keys), (value_acc, to_values)):
                sums_of = [
                    acc[slot] + part[index * SPAN : (index + 1) * SPAN]
                    for index, slot in enumerate(slots)
                ]
                for slot, total in zip(slots, sums_of):
                    acc[slot] = total
        return 0

    for unit in range(4):
        both[unit, 1] = (dq[unit] * SCALE).astype(BF16)
    both_store = pltpu.make_async_copy(both, both_out, out_sem.at[2 * NZ])
    both_store.start()
    stores = [both_store]
    for index in range(2 * NZ):
        for part in range(4):
            kv[index, 0, part] = (key_acc[index * 4 + part] * SCALE).astype(BF16)
            kv[index, 1, part] = value_acc[index * 4 + part].astype(BF16)
        store = pltpu.make_async_copy(kv.at[index], dkv.at[index], out_sem.at[index])
        store.start()
        stores.append(store)
    for store in stores:
        store.wait()


def attend(order, docs, q_cols, g_cols, q_rows, g_rows, kv):
    return pl.pallas_call(
        attend_kernel,
        out_shape=(
            jax.ShapeDtypeStruct((4, 2, HD, LANES), BF16),
            jax.ShapeDtypeStruct((2 * NZ, 2, 4, SPAN, HD), BF16),
        ),
        in_specs=[HBM] * 7,
        out_specs=(HBM,) * 2,
        scratch_shapes=[
            pltpu.SMEM((2 * SLOTS,), jnp.int32),
            pltpu.VMEM((SLOTS, ROWS), jnp.int32),
            pltpu.VMEM((4, HD, LANES), BF16),
            pltpu.VMEM((4, HD, LANES), BF16),
            pltpu.VMEM((4, LANES, HD), BF16),
            pltpu.VMEM((4, LANES, HD), BF16),
            pltpu.VMEM((4, 2, HD, LANES), BF16),
            pltpu.VMEM((4, HD, LANES), F32),
            pltpu.VMEM((2 * NZ + 1, 2, 4, SPAN, HD), BF16),
            pltpu.VMEM((4 * SLOTS // ITEM, ITEM * SPAN, LANES), F32),
            pltpu.VMEM((SLOTS + 1, SPAN, HD), F32),
            pltpu.VMEM((SLOTS + 1, SPAN, HD), F32),
            pltpu.VMEM((4, HD, LANES), F32),
            pltpu.VMEM((4, 8, LANES), F32),
            pltpu.VMEM((4, 8, LANES), F32),
            pltpu.VMEM((4, 8, LANES), F32),
            pltpu.VMEM((4, 8, LANES), F32),
            pltpu.VMEM((4, 8, ROWS), jnp.int32),
            pltpu.VMEM((4, 8, ROWS), jnp.int32),
            pltpu.SMEM((80,), jnp.int32),
            pltpu.SMEM((512,), jnp.int32),
            pltpu.SemaphoreType.DMA((8,)),
            pltpu.SemaphoreType.DMA((2 * NZ + 1,)),
        ],
        compiler_params=pltpu.CompilerParams(vmem_limit_bytes=60 << 20),
        cost_estimate=pl.CostEstimate(
            flops=6 * 2 * 2048 * 2048 * HD, bytes_accessed=12 << 20, transcendentals=2048 * 2048
        ),
        name="attend",
    )(order, docs, q_cols, g_cols, q_rows, g_rows, kv)


def return_kernel(
    both_in, dkv, both_out, dkv_out,
    both, terms, both_rows, order, landed, landed_rows, final, pair_send, pair_recv, own_sem, l_send, l_recv, r_send, r_recv,
):
    x, y, z, core = place()
    sibling = where_is(x, y, z, 1 - core)
    up = where_is(x, y, lax.rem(z + 1, NZ), core)
    down = where_is(x, y, lax.rem(z + NZ - 1, NZ), core)
    later = where_is(x, lax.rem(y + 1, NY), z, core)
    earlier = where_is(x, lax.rem(y + NY - 1, NY), z, core)
    loads = [
        pltpu.make_async_copy(both_in, both, own_sem.at[5]),
        pltpu.make_async_copy(dkv, terms, own_sem.at[4]),
    ]
    for load in loads:
        load.start()
    up_z, down_z = lax.rem(z + 1, NZ), lax.rem(z + NZ - 1, NZ)
    later_y, earlier_y = lax.rem(y + 1, NY), lax.rem(y + NY - 1, NY)
    corners = (where_is(x, earlier_y, up_z, core), where_is(x, earlier_y, down_z, core))
    behind = [where_is(x, later_y, up_z, core), where_is(x, later_y, down_z, core)]
    across = [
        where_is(x, y, up_z, 1 - core),
        where_is(x, y, down_z, 1 - core),
        where_is(x, earlier_y, z, 1 - core),
    ]
    greet(
        [sibling, up, down, later, earlier, *corners, *behind, *across]
        + [where_is(x, later_y, z, 1 - core)]
    )

    ways = (up, down)
    sent = []

    def at(group, distance, way):
        return group * NZ + lax.rem(z + NZ + distance * (-1 if way else 1), NZ)

    def ship(src, index, partner):
        copy = send(src, landed.at[index], l_send.at[index], l_recv.at[index], partner)
        sent.append(copy)
        return copy

    def add(block, kind, *indices):
        total = terms[block, kind].astype(F32)
        for index in indices:
            total = total + landed[index].astype(F32)
        terms[block, kind] = total.astype(BF16)

    mine = pl.ds(pl.multiple_of(core * ROWS, ROWS), ROWS)
    other = pl.ds(pl.multiple_of((1 - core) * ROWS, ROWS), ROWS)

    def deliver(block, kind, index, straight, crossed):
        copies = []
        for half, rows, partner in ((0, mine, straight), (1, other, crossed)):
            copy = send(
                terms.at[block, kind, rows], landed_rows.at[half, index],
                r_send.at[half, index], r_recv.at[half, index], partner,
            )
            sent.append(copy)
            copies.append(copy)
        return copies

    flying = {}
    for way in range(2):
        flying["s", 1, way, way] = ship(dkv.at[at(0, 4, 0), way], 16 + way, ways[way])
    for step, distance in ((0, 3), (1, 1)):
        for kind in range(2):
            for way in range(2):
                if step == 1 and kind == way:
                    continue
                flying["z", step, way, kind] = ship(
                    dkv.at[at(1, distance, way), kind], step * 4 + way * 2 + kind, ways[way]
                )
        if step == 0:
            for kind in range(2):
                flying["y", 4, kind] = ship(dkv.at[at(1, 4, 0), kind], 8 + kind, corners[kind])
    swaps = []
    own = []

    def turn(block, half):
        stacked = both[2 * block + half].reshape(2 * HD, LANES)
        rows = lax.dot_general(
            order[...], stacked, (((1,), (1,)), ((), ())), preferred_element_type=F32
        ).astype(BF16)
        for kind in range(2):
            both_rows[block, kind, half * LANES : (half + 1) * LANES, :] = rows[
                :, kind * HD : (kind + 1) * HD
            ]

    def swap():
        swaps.append(
            send(
                both_rows.at[1 - core], both_out.at[core], pair_send.at[0], pair_recv.at[0], sibling
            )
        )

    def stay():
        copy = pltpu.make_async_copy(both_rows.at[core], both_out.at[core], own_sem.at[0])
        copy.start()
        own.append(copy)

    row = lax.broadcasted_iota(jnp.int32, (LANES, LANES), 0)
    lane = lax.broadcasted_iota(jnp.int32, (LANES, LANES), 1)
    from_lane = lax.rem(row, GROUP) * SPAN + lax.div(row, GROUP)
    order[...] = jnp.where(lane == from_lane, 1.0, 0.0).astype(BF16)
    loads[1].wait()
    for kind in range(2):
        for way in range(2):
            flying["z", 0, way, kind].wait_recv()
            block = at(1, 2, way)
            add(block, kind, way * 2 + kind)
            flying["y", 2, way, kind] = ship(
                terms.at[block, kind], 10 + way * 2 + kind, earlier
            )
    for way in range(2):
        flying["y", 1, way] = ship(dkv.at[at(1, 1, way), way], 30 + way, earlier)
    for way in range(2):
        kind = 1 - way
        flying["s", 2, way, kind] = ship(
            terms.at[at(0, 3, way), kind], 18 + way * 2 + kind, ways[way]
        )
    loads[0].wait()
    turn(1 - core, 0)
    for kind in range(2):
        swaps.append(
            send(
                dkv.at[z, kind, other], landed_rows.at[1, 6 + kind],
                r_send.at[1, 6 + kind], r_recv.at[1, 6 + kind], sibling,
            )
        )
    for way in range(2):
        flying["s", 1, way, way].wait_recv()
        flying["y", 4, way].wait_recv()
        add(at(0, 3, way), way, 16 + way, 8 + way)
        flying["s", 2, way, way] = ship(
            terms.at[at(0, 3, way), way], 18 + way * 2 + way, ways[way]
        )
    for kind in range(2):
        way = 1 - kind
        flying["z", 1, way, kind].wait_recv()
        add(NZ + z, kind, 4 + way * 2 + kind)
        flying["y", 0, kind] = deliver(NZ + z, kind, kind, earlier, across[2])
    turn(1 - core, 1)
    swap()
    for step in (3, 4):
        for turn_of in range(2):
            for way in range(2):
                kind = turn_of if way else 1 - turn_of
                flying["s", step - 1, way, kind].wait_recv()
                indices = [18 + (step - 3) * 4 + way * 2 + kind]
                if step == 3:
                    flying["y", 2, way, kind].wait_recv()
                    indices.append(10 + way * 2 + kind)
                elif kind == way:
                    flying["y", 1, way].wait_recv()
                    indices.append(30 + way)
                block = at(0, 5 - step, way)
                add(block, kind, *indices)
                if step == 3:
                    flying["s", step, way, kind] = ship(
                        terms.at[block, kind], 22 + way * 2 + kind, ways[way]
                    )
                else:
                    flying["s", step, way, kind] = deliver(
                        block, kind, 2 + way * 2 + kind, ways[way], across[way]
                    )
        turn(core, step - 3)
    stay()
    for kind in range(2):
        for half in range(2):
            flying["y", 0, kind][half].wait_recv()
            for way in range(2):
                flying["s", 4, way, kind][half].wait_recv()
            if half:
                swaps[kind].wait_recv()
                total = landed_rows[1, 6 + kind].astype(F32)
            else:
                total = terms[z, kind, mine].astype(F32)
            for index in (kind, 2 + kind, 4 + kind):
                total = total + landed_rows[half, index].astype(F32)
            final[kind, half] = total
        for half in range(2):
            copy = pltpu.make_async_copy(
                final.at[kind, half], dkv_out.at[kind, core if half == 0 else 1 - core],
                own_sem.at[2 + (0, 5)[half] + kind],
            )
            copy.start()
            own.append(copy)
    for copy in sent:
        copy.wait_send()
    for copy in swaps[:2]:
        copy.wait_send()
    swaps[2].wait()
    for copy in own:
        copy.wait()


def give_back(both, dkv):
    return pl.pallas_call(
        return_kernel,
        out_shape=(
            jax.ShapeDtypeStruct((2, 2, ROWS * GROUP, HD), BF16),
            jax.ShapeDtypeStruct((2, 2, ROWS, HD), F32),
        ),
        in_specs=[HBM] * 2,
        out_specs=(HBM,) * 2,
        scratch_shapes=[
            pltpu.VMEM((4, 2, HD, LANES), BF16),
            pltpu.VMEM((2 * NZ, 2, 2 * ROWS, HD), BF16),
            pltpu.VMEM((2, 2, ROWS * GROUP, HD), BF16),
            pltpu.VMEM((LANES, LANES), BF16),
            pltpu.VMEM((32, 2 * ROWS, HD), BF16),
            pltpu.VMEM((2, 8, ROWS, HD), BF16),
            pltpu.VMEM((2, 2, ROWS, HD), F32),
            pltpu.SemaphoreType.DMA((1,)),
            pltpu.SemaphoreType.DMA((1,)),
            pltpu.SemaphoreType.DMA((9,)),
            pltpu.SemaphoreType.DMA((32,)),
            pltpu.SemaphoreType.DMA((32,)),
            pltpu.SemaphoreType.DMA((2, 8)),
            pltpu.SemaphoreType.DMA((2, 8)),
        ],
        compiler_params=pltpu.CompilerParams(
            collective_id=1, has_side_effects=True, vmem_limit_bytes=60 << 20
        ),
        name="give_back",
    )(both, dkv)


def finish_kernel(
    both, dkv, attn_out, dq_out, dk_out, dv_out, halves, attn, dq, parts, dk, dv, sem
):
    loads = [pltpu.make_async_copy(dkv, parts, sem.at[0])]
    for kind in range(2):
        loads.append(
            pltpu.make_async_copy(both.at[:, kind], halves.at[:, kind], sem.at[1 + kind])
        )
    for load in loads:
        load.start()
    stores = []
    loads[0].wait()
    for kind, (rows, dst) in enumerate(((dk, dk_out), (dv, dv_out))):
        for half in range(2):
            rows[pl.ds(half, ROWS, stride=2), :] = parts[kind, half]
        store = pltpu.make_async_copy(rows, dst, sem.at[3 + kind])
        store.start()
        stores.append(store)
    for kind, (joined, dst) in ((1, (dq, dq_out)), (0, (attn, attn_out))):
        loads[1 + kind].wait()
        pair = [halves[half, kind].astype(F32).reshape(ROWS, GROUP, HD) for half in range(2)]
        joined[...] = jnp.concatenate(pair, axis=1).astype(joined.dtype)
        store = pltpu.make_async_copy(joined, dst, sem.at[5 + kind])
        store.start()
        stores.append(store)
    for store in stores:
        store.wait()


def finish(both, dkv):
    return pl.pallas_call(
        finish_kernel,
        out_shape=(
            jax.ShapeDtypeStruct((ROWS, 2 * GROUP, HD), BF16),
            jax.ShapeDtypeStruct((ROWS, 2 * GROUP, HD), F32),
            jax.ShapeDtypeStruct((2 * ROWS, HD), F32),
            jax.ShapeDtypeStruct((2 * ROWS, HD), F32),
        ),
        in_specs=[HBM] * 2,
        out_specs=(HBM,) * 4,
        scratch_shapes=[
            pltpu.VMEM((2, 2, ROWS * GROUP, HD), BF16),
            pltpu.VMEM((ROWS, 2 * GROUP, HD), BF16),
            pltpu.VMEM((ROWS, 2 * GROUP, HD), F32),
            pltpu.VMEM((2, 2, ROWS, HD), F32),
            pltpu.VMEM((2 * ROWS, HD), F32),
            pltpu.VMEM((2 * ROWS, HD), F32),
            pltpu.SemaphoreType.DMA((7,)),
        ],
        compiler_params=pltpu.CompilerParams(vmem_limit_bytes=60 << 20),
        cost_estimate=pl.CostEstimate(flops=0, bytes_accessed=4 << 20, transcendentals=0),
        name="finish",
    )(both, dkv)


def local(queries, keys, values, grad_out, span_order, doc_ids):
    turned = [jnp.transpose(a, (1, 2, 0)) for a in (queries, keys, values, grad_out)]
    q_cols, g_cols, q_rows, g_rows, kv = bring(*turned)
    kv = kv.reshape(2 * NZ, 2, 4, SPAN, HD)
    both, dkv = attend(
        span_order, doc_ids.reshape(SLOTS, ROWS), q_cols, g_cols, q_rows, g_rows, kv
    )
    both, dkv = give_back(both, dkv.reshape(2 * NZ, 2, 2 * ROWS, HD))
    attn, dq, dk, dv = finish(both, dkv)
    return (attn, dq, dk.reshape(ROWS, 2, HD), dv.reshape(ROWS, 2, HD))


def solution(mesh):
    entry = P(("outer", "inner"), None, "head")
    leave = P(("outer", "inner"), "head", None)
    return jax.shard_map(
        local,
        mesh=mesh,
        in_specs=(entry, entry, entry, entry, P(), P()),
        out_specs=(leave, leave, leave, leave),
        check_vma=False,
    )
```

profile of v0, /device:TPU:1, one launch (start us, length us, event | category | flops | bytes accessed | tf_op | source)
XLA Modules:
  0.0 80.0 jit_solution(9395676117775524180)
XLA Ops:
  0.6 34.7 %bring.1 = (bf16[4,128,512]{2,1,0:T(8,128)(2,1)}, bf16[4,128,512]{2,1,0:T(8,128)(2,1)}, bf16[4,512,128]{2,1,0:T(8,128)(2,1)}, bf16[4,512,128]{2,1,0:T(8,128)(2,1)}, bf16[16,2,256,128]{3,2,1,0:T(8,128)(2,1)}) custom-call(bf16[64,32,128]{2,1,0:T(8,128)(2,1)} %bitcast.10, bf16[8,32,128]{2,1,0:T(8,128)(2,1)} %bitcast.12, bf16[8,32,128]{2,1,0:T(8,128)(2,1)} %bitcast.13, ...), custom_call_target="tpu_custom_call" | custom-call | tf_op jit(solution)/shard_map/bring/pallas_call | solution.py:275
  35.3 14.6 %attend.1 = (bf16[4,2,128,512]{3,2,1,0:T(8,128)(2,1)}, bf16[16,2,4,64,128]{4,3,2,1,0:T(8,128)(2,1)}) custom-call(s32[128]{0:T(128)} %order_in.1, s32[64,128]{1,0:T(8,128)} %bitcast.17, bf16[4,128,512]{2,1,0:T(8,128)(2,1)} %get-tuple-element.17.q_cols_in, bf16[4,128,512]{2,1,0:T(8,128)(2,1)} %get-tuple-element.18.g_cols_in, ...), custom_call_target="tpu_custom_call" | custom-call | flops 6442450944 | bytes 12582912 | tf_op jit(solution)/shard_map/attend/pallas_call | solution.py:528
  49.9 27.5 %give_back.1 = (bf16[2,2,1024,128]{3,2,1,0:T(8,128)(2,1)}, f32[2,2,128,128]{3,2,1,0:T(8,128)}) custom-call(bf16[4,2,128,512]{3,2,1,0:T(8,128)(2,1)} %get-tuple-element.22.both_in, bf16[16,2,256,128]{3,2,1,0:T(8,128)(2,1)} %bitcast.9), custom_call_target="tpu_custom_call" | custom-call | tf_op jit(solution)/shard_map/give_back/pallas_call | solution.py:766
  77.4 2.5 %finish.1 = (bf16[128,16,128]{2,1,0:T(8,128)(2,1)}, f32[128,16,128]{2,1,0:T(8,128)}, f32[256,128]{1,0:T(8,128)}, f32[256,128]{1,0:T(8,128)}) custom-call(bf16[2,2,1024,128]{3,2,1,0:T(8,128)(2,1)} %get-tuple-element.24.both, f32[2,2,128,128]{3,2,1,0:T(8,128)} %get-tuple-element.25.dkv), custom_call_target="tpu_custom_call" | custom-call | bytes 4194304 | tf_op jit(solution)/shard_map/finish/pallas_call | solution.py:827
where the time goes:
time: 80.2 us; the launch traced here: 80 us
  Pallas kernels  79.3 us (99%)
    pallas_call x1, Pallas kernels, bring(): pl.pallas_call(bring_kernel, out_shape=(jax.ShapeDtypeStruct((4, HD, LANE...  34.7 us
    pallas_call x1, Pallas kernels, give_back(): pl.pallas_call(return_kernel, out_shape=(jax.ShapeDtypeStruct((2, 2, ROWS...  27.5 us
    pallas_call x1, Pallas kernels, attend(): pl.pallas_call(attend_kernel, out_shape=(jax.ShapeDtypeStruct((4, 2, HD,...  14.6 us
    pallas_call x1, Pallas kernels, finish(): pl.pallas_call(finish_kernel, out_shape=(jax.ShapeDtypeStruct((ROWS, 2 *...  2.55 us

commit v1 on v0

--- a/solution.py
+++ b/solution.py
@@ -64,7 +64,7 @@
 
 def bring_kernel(
     q, k, v, g, q_cols_out, g_cols_out, q_rows_out, g_rows_out, kv_out,
-    q_cols, g_cols, q_rows, g_rows, out_sem, q_in, g_in, kv_in, ring_kv, relay, relay_sem, own_sem, keep_sem, x_send, x_recv, y_send, y_recv, z_send, z_recv,
+    q_cols, g_cols, q_rows, g_rows, out_sem, q_in, g_in, kv_in, ring_kv, own_sem, keep_sem, x_send, x_recv, y_send, y_recv, z_send, z_recv,
 ):
     x, y, z, core = place()
     peers = [(dx, dc) for dx in range(NX) for dc in range(2) if (dx, dc) != (0, 0)]
@@ -183,17 +183,11 @@
         copy.start()
         own.append(copy)
     wide = ([], [])
-    relays = []
-    for kind, src in enumerate((q, g)):
-        relays.append(
-            send(
-                src.at[pl.ds(lax.rem(x + 2, NX) * 2 * GROUP, 2 * GROUP)], relay.at[kind],
-                relay_sem.at[0, kind], relay_sem.at[1, kind], peer(3 if kind else 1, 0),
-            )
-        )
-    for kind, (src, dst) in enumerate(((q, q_in), (g, g_in))):
+
+    def spread(kind, *offsets):
+        src, dst = ((q, q_in), (g, g_in))[kind]
         for index, (dx, dc) in enumerate(peers):
-            if dx == 2:
+            if dx not in offsets:
                 continue
             head = lax.rem(x + dx, NX) * 2 + lax.rem(core + dc, 2)
             wide[kind].append(
@@ -205,23 +199,9 @@
                     peer(dx, dc),
                 )
             )
-    def forward(kind):
-        relays[kind].wait_recv()
-        from_x = lax.rem(x + (1 if kind else 3), NX)
-        for index, (dx, dc) in enumerate(peers):
-            if dx != 2:
-                continue
-            head = pl.ds(lax.rem(core + dc, 2) * GROUP, GROUP)
-            wide[kind].append(
-                send(
-                    relay.at[kind, head],
-                    (q_in, g_in)[kind].at[core, from_x],
-                    x_send.at[2 + kind, index],
-                    x_recv.at[2 + kind, index],
-                    peer(3 if kind else 1, dc),
-                )
-            )
-
+
+    spread(0, 2)
+    spread(0, 0, 1)
     far_shift = {}
     for step in range(1, 4):
         for kind in range(2):
@@ -236,8 +216,10 @@
         for way in range(2):
             keep(block_at(0, way, step), 1 + 2 * step + way)
         if step == 1:
-            forward(0)
-            forward(1)
+            spread(0, 3)
+            spread(1, 2)
+        elif step == 2:
+            spread(1, 0, 1, 3)
     hops = {}
     for kind in range(2):
         self_shift[kind].wait_recv()
@@ -263,7 +245,7 @@
     for way in range(2):
         far_shift[way, 4].wait_recv()
     keep(block_at(1, 0, 4), 15)
-    for copy in sent + relays:
+    for copy in sent:
         copy.wait_send()
     for copy in keeps:
         copy.wait()
@@ -293,8 +275,6 @@
             pltpu.VMEM((2, NX, GROUP, HD // NX, ROWS), BF16),
             pltpu.VMEM((2, 2, HD, ROWS), BF16),
             pltpu.VMEM((2 * NZ, 2, 2 * ROWS, HD), BF16),
-            pltpu.VMEM((2, 2 * GROUP, HD // NX, ROWS), BF16),
-            pltpu.SemaphoreType.DMA((2, 2)),
             pltpu.SemaphoreType.DMA((4,)),
             pltpu.SemaphoreType.DMA((16,)),
             pltpu.SemaphoreType.DMA((4, 8)),
@@ -708,7 +688,6 @@
         add(NZ + z, kind, 4 + way * 2 + kind)
         flying["y", 0, kind] = deliver(NZ + z, kind, kind, earlier, across[2])
     turn(1 - core, 1)
-    swap()
     for step in (3, 4):
         for turn_of in range(2):
             for way in range(2):
@@ -731,8 +710,12 @@
                     flying["s", step, way, kind] = deliver(
                         block, kind, 2 + way * 2 + kind, ways[way], across[way]
                     )
-        turn(core, step - 3)
-    stay()
+        if step == 3:
+            turn(core, 0)
+        else:
+            swap()
+            turn(core, 1)
+            stay()
     for kind in range(2):
         for half in range(2):
             flying["y", 0, kind][half].wait_recv()

time: 80.2 us -> 80.1 us (level)
    pallas_call x1, Pallas kernels: 14.6 us -> 10.4 us  [attend(): pl.pallas_call(attend_kernel, out_shape=(jax.ShapeDtypeStruct((4, 2, HD,...]
    pallas_call x1, Pallas kernels: 27.5 us -> 31.5 us  [give_back(): pl.pallas_call(return_kernel, out_shape=(jax.ShapeDtypeStruct((2, 2, ROWS...]
where the time goes in v1:
time: 80.1 us; the launch traced here: 79.9 us
  Pallas kernels  79.2 us (99%)
    pallas_call x1, Pallas kernels, bring(): pl.pallas_call(bring_kernel, out_shape=(jax.ShapeDtypeStruct((4, HD, LANE...  34.8 us
    pallas_call x1, Pallas kernels, give_back(): pl.pallas_call(return_kernel, out_shape=(jax.ShapeDtypeStruct((2, 2, ROWS...  31.5 us
    pallas_call x1, Pallas kernels, attend(): pl.pallas_call(attend_kernel, out_shape=(jax.ShapeDtypeStruct((4, 2, HD,...  10.4 us
    pallas_call x1, Pallas kernels, finish(): pl.pallas_call(finish_kernel, out_shape=(jax.ShapeDtypeStruct((ROWS, 2 *...  2.55 us

profile of v1, /device:TPU:1, one launch (start us, length us, event | category | flops | bytes accessed | tf_op | source)
XLA Modules:
  0.0 79.9 jit_solution(13897056663354637123)
XLA Ops:
  0.6 34.8 %bring.1 = (bf16[4,128,512]{2,1,0:T(8,128)(2,1)}, bf16[4,128,512]{2,1,0:T(8,128)(2,1)}, bf16[4,512,128]{2,1,0:T(8,128)(2,1)}, bf16[4,512,128]{2,1,0:T(8,128)(2,1)}, bf16[16,2,256,128]{3,2,1,0:T(8,128)(2,1)}) custom-call(bf16[64,32,128]{2,1,0:T(8,128)(2,1)} %bitcast.10, bf16[8,32,128]{2,1,0:T(8,128)(2,1)} %bitcast.12, bf16[8,32,128]{2,1,0:T(8,128)(2,1)} %bitcast.13, ...), custom_call_target="tpu_custom_call" | custom-call | tf_op jit(solution)/shard_map/bring/pallas_call | solution.py:257
  35.4 10.4 %attend.1 = (bf16[4,2,128,512]{3,2,1,0:T(8,128)(2,1)}, bf16[16,2,4,64,128]{4,3,2,1,0:T(8,128)(2,1)}) custom-call(s32[128]{0:T(128)} %order_in.1, s32[64,128]{1,0:T(8,128)} %bitcast.17, bf16[4,128,512]{2,1,0:T(8,128)(2,1)} %get-tuple-element.17.q_cols_in, bf16[4,128,512]{2,1,0:T(8,128)(2,1)} %get-tuple-element.18.g_cols_in, ...), custom_call_target="tpu_custom_call" | custom-call | flops 6442450944 | bytes 12582912 | tf_op jit(solution)/shard_map/attend/pallas_call | solution.py:508
  45.8 31.5 %give_back.1 = (bf16[2,2,1024,128]{3,2,1,0:T(8,128)(2,1)}, f32[2,2,128,128]{3,2,1,0:T(8,128)}) custom-call(bf16[4,2,128,512]{3,2,1,0:T(8,128)(2,1)} %get-tuple-element.22.both_in, bf16[16,2,256,128]{3,2,1,0:T(8,128)(2,1)} %bitcast.9), custom_call_target="tpu_custom_call" | custom-call | tf_op jit(solution)/shard_map/give_back/pallas_call | solution.py:749
  77.4 2.5 %finish.1 = (bf16[128,16,128]{2,1,0:T(8,128)(2,1)}, f32[128,16,128]{2,1,0:T(8,128)}, f32[256,128]{1,0:T(8,128)}, f32[256,128]{1,0:T(8,128)}) custom-call(bf16[2,2,1024,128]{3,2,1,0:T(8,128)(2,1)} %get-tuple-element.24.both, f32[2,2,128,128]{3,2,1,0:T(8,128)} %get-tuple-element.25.dkv), custom_call_target="tpu_custom_call" | custom-call | bytes 4194304 | tf_op jit(solution)/shard_map/finish/pallas_call | solution.py:810

commit v2 on v1

--- a/solution.py
+++ b/solution.py
@@ -42,10 +42,11 @@
     return {"head": x, "outer": y, "inner": z * 2 + core}
 
 
-def greet(partners):
+def greet(partners, meanwhile):
     barrier = pltpu.get_barrier_semaphore()
     for partner in partners:
         pl.semaphore_signal(barrier, inc=1, device_id=partner, device_id_type=MESH)
+    meanwhile()
     pl.semaphore_wait(barrier, len(partners))
 
 
@@ -64,7 +65,7 @@
 
 def bring_kernel(
     q, k, v, g, q_cols_out, g_cols_out, q_rows_out, g_rows_out, kv_out,
-    q_cols, g_cols, q_rows, g_rows, out_sem, q_in, g_in, kv_in, ring_kv, own_sem, keep_sem, x_send, x_recv, y_send, y_recv, z_send, z_recv,
+    q_cols, g_cols, q_rows, g_rows, out_sem, swap, q_in, g_in, kv_in, ring_kv, own_sem, keep_sem, x_send, x_recv, y_send, y_recv, z_send, z_recv,
 ):
     x, y, z, core = place()
     peers = [(dx, dc) for dx in range(NX) for dc in range(2) if (dx, dc) != (0, 0)]
@@ -80,7 +81,14 @@
     later_y, earlier_y = lax.rem(y + 1, NY), lax.rem(y + NY - 1, NY)
     corners = (where_is(x, later_y, up_z, core), where_is(x, later_y, down_z, core))
     behind = [where_is(x, earlier_y, up_z, core), where_is(x, earlier_y, down_z, core)]
-    greet([peer(*p) for p in peers] + [up, down, later, earlier, *corners, *behind])
+    def prepare():
+        row = lax.broadcasted_iota(jnp.int32, (2 * ROWS, 2 * ROWS), 0)
+        lane = lax.broadcasted_iota(jnp.int32, (2 * ROWS, 2 * ROWS), 1)
+        middle = (row >= SPAN) & (row < 3 * SPAN)
+        swapped = jnp.where(row < ROWS, row + SPAN, row - SPAN)
+        swap[...] = jnp.where(lane == jnp.where(middle, swapped, row), 1.0, 0.0).astype(BF16)
+
+    greet([peer(*p) for p in peers] + [up, down, later, earlier, *corners, *behind], prepare)
 
     here = pl.ds(pl.multiple_of(x * 32, 32), 32)
     copies = []
@@ -143,24 +151,24 @@
         own[2 + kind].wait()
         for copy in wide[kind]:
             copy.wait()
-        low = lax.broadcasted_iota(jnp.int32, (HD, ROWS), 1) < SPAN
-
-        @pl.loop(0, 8)
-        def _(index):
-            block = lax.div(index, 4)
-            pair = lax.rem(index, 4)
-            lanes = pl.ds(pl.multiple_of(pair * ROWS, ROWS), ROWS)
-            first, second = [
-                jnp.concatenate([src[block, a, 2 * pair + b] for a in range(NX)], axis=0).astype(F32)
-                for b in range(2)
-            ]
-            halves = (
-                jnp.where(low, first, pltpu.roll(second, SPAN, 1)),
-                jnp.where(low, pltpu.roll(first, SPAN, 1), second),
-            )
-            for half in range(2):
-                cols[2 * block + half, :, lanes] = halves[half].astype(BF16)
-                rows[2 * block + half, lanes, :] = halves[half].T.astype(BF16)
+        for block in range(2):
+            for pair in range(4):
+                lanes = pl.ds(pair * ROWS, ROWS)
+                both = jnp.concatenate(
+                    [
+                        jnp.concatenate([src[block, a, 2 * pair + b] for a in range(NX)], axis=0)
+                        for b in range(2)
+                    ],
+                    axis=1,
+                )
+                across = jnp.dot(both, swap[...], preferred_element_type=F32).astype(BF16)
+                along = lax.dot_general(
+                    swap[...], both, (((1,), (1,)), ((), ())), preferred_element_type=F32
+                ).astype(BF16)
+                for half in range(2):
+                    part = slice(half * ROWS, (half + 1) * ROWS)
+                    cols[2 * block + half, :, lanes] = across[:, part]
+                    rows[2 * block + half, lanes, :] = along[part]
 
         outs = ((q_cols_out, q_rows_out), (g_cols_out, g_rows_out))[kind]
         for index, (src, dst) in enumerate(zip((cols, rows), outs)):
@@ -271,6 +279,7 @@
             pltpu.VMEM((4, LANES, HD), BF16),
             pltpu.VMEM((4, LANES, HD), BF16),
             pltpu.SemaphoreType.DMA((2, 2)),
+            pltpu.VMEM((2 * ROWS, 2 * ROWS), BF16),
             pltpu.VMEM((2, NX, GROUP, HD // NX, ROWS), BF16),
             pltpu.VMEM((2, NX, GROUP, HD // NX, ROWS), BF16),
             pltpu.VMEM((2, 2, HD, ROWS), BF16),
@@ -571,9 +580,16 @@
         where_is(x, y, down_z, 1 - core),
         where_is(x, earlier_y, z, 1 - core),
     ]
+    def prepare():
+        row = lax.broadcasted_iota(jnp.int32, (LANES, LANES), 0)
+        lane = lax.broadcasted_iota(jnp.int32, (LANES, LANES), 1)
+        from_lane = (row & (GROUP - 1)) * SPAN + (row >> 3)
+        order[...] = jnp.where(lane == from_lane, 1.0, 0.0).astype(BF16)
+
     greet(
         [sibling, up, down, later, earlier, *corners, *behind, *across]
-        + [where_is(x, later_y, z, 1 - core)]
+        + [where_is(x, later_y, z, 1 - core)],
+        prepare,
     )
 
     ways = (up, down)
@@ -646,10 +662,6 @@
         copy.start()
         own.append(copy)
 
-    row = lax.broadcasted_iota(jnp.int32, (LANES, LANES), 0)
-    lane = lax.broadcasted_iota(jnp.int32, (LANES, LANES), 1)
-    from_lane = lax.rem(row, GROUP) * SPAN + lax.div(row, GROUP)
-    order[...] = jnp.where(lane == from_lane, 1.0, 0.0).astype(BF16)
     loads[1].wait()
     for kind in range(2):
         for way in range(2):

time: 80.1 us -> 81.7 us (1.020)
  Pallas kernels: 79.2 us -> 80.8 us
    pallas_call x1, Pallas kernels: 10.4 us -> 12.5 us  [attend(): pl.pallas_call(attend_kernel, out_shape=(jax.ShapeDtypeStruct((4, 2, HD,...]
where the time goes in v2:
time: 81.7 us; the launch traced here: 81.4 us
  Pallas kernels  80.8 us (99%)
    pallas_call x1, Pallas kernels, bring(): pl.pallas_call(bring_kernel, out_shape=(jax.ShapeDtypeStruct((4, HD, LANE...  34.8 us
    pallas_call x1, Pallas kernels, give_back(): pl.pallas_call(return_kernel, out_shape=(jax.ShapeDtypeStruct((2, 2, ROWS...  31 us
    pallas_call x1, Pallas kernels, attend(): pl.pallas_call(attend_kernel, out_shape=(jax.ShapeDtypeStruct((4, 2, HD,...  12.5 us
    pallas_call x1, Pallas kernels, finish(): pl.pallas_call(finish_kernel, out_shape=(jax.ShapeDtypeStruct((ROWS, 2 *...  2.55 us

profile of v2, /device:TPU:1, one launch (start us, length us, event | category | flops | bytes accessed | tf_op | source)
XLA Modules:
  0.0 81.4 jit_solution(6683343440301003484)
XLA Ops:
  0.6 34.8 %bring.1 = (bf16[4,128,512]{2,1,0:T(8,128)(2,1)}, bf16[4,128,512]{2,1,0:T(8,128)(2,1)}, bf16[4,512,128]{2,1,0:T(8,128)(2,1)}, bf16[4,512,128]{2,1,0:T(8,128)(2,1)}, bf16[16,2,256,128]{3,2,1,0:T(8,128)(2,1)}) custom-call(bf16[64,32,128]{2,1,0:T(8,128)(2,1)} %bitcast.10, bf16[8,32,128]{2,1,0:T(8,128)(2,1)} %bitcast.12, bf16[8,32,128]{2,1,0:T(8,128)(2,1)} %bitcast.13, ...), custom_call_target="tpu_custom_call" | custom-call | tf_op jit(solution)/shard_map/bring/pallas_call | solution.py:265
  35.4 12.5 %attend.1 = (bf16[4,2,128,512]{3,2,1,0:T(8,128)(2,1)}, bf16[16,2,4,64,128]{4,3,2,1,0:T(8,128)(2,1)}) custom-call(s32[128]{0:T(128)} %order_in.1, s32[64,128]{1,0:T(8,128)} %bitcast.17, bf16[4,128,512]{2,1,0:T(8,128)(2,1)} %get-tuple-element.17.q_cols_in, bf16[4,128,512]{2,1,0:T(8,128)(2,1)} %get-tuple-element.18.g_cols_in, ...), custom_call_target="tpu_custom_call" | custom-call | flops 6442450944 | bytes 12582912 | tf_op jit(solution)/shard_map/attend/pallas_call | solution.py:517
  47.9 31.0 %give_back.1 = (bf16[2,2,1024,128]{3,2,1,0:T(8,128)(2,1)}, f32[2,2,128,128]{3,2,1,0:T(8,128)}) custom-call(bf16[4,2,128,512]{3,2,1,0:T(8,128)(2,1)} %get-tuple-element.22.both_in, bf16[16,2,256,128]{3,2,1,0:T(8,128)(2,1)} %bitcast.9), custom_call_target="tpu_custom_call" | custom-call | tf_op jit(solution)/shard_map/give_back/pallas_call | solution.py:761
  78.9 2.5 %finish.1 = (bf16[128,16,128]{2,1,0:T(8,128)(2,1)}, f32[128,16,128]{2,1,0:T(8,128)}, f32[256,128]{1,0:T(8,128)}, f32[256,128]{1,0:T(8,128)}) custom-call(bf16[2,2,1024,128]{3,2,1,0:T(8,128)(2,1)} %get-tuple-element.24.both, f32[2,2,128,128]{3,2,1,0:T(8,128)} %get-tuple-element.25.dkv), custom_call_target="tpu_custom_call" | custom-call | bytes 4194304 | tf_op jit(solution)/shard_map/finish/pallas_call | solution.py:822
